TPU v7x, 128 devices: a whole 4x4x4 slice. The times are simulated.
128 devices in a mesh: occ: 64 (over z_lo, x, y, core), aux: 2 (over z_hi).
Axes of the slice: x: 4, y: 4, z: 4 (z_hi: 2, z_lo: 2; z = z_hi * 2 + z_lo), core: 2. Of those that a mesh axis runs over, the one named last changes fastest.
Arguments:
- occ_energy: float32 [256], replicated, may hold values from -2 to -0.3
- vir_energy: float32 [512], replicated, may hold values from 0.2 to 3
- factors: bfloat16 [256, 512, 2048], P(('occ', 'aux')), may hold values from -3.5 to 3.5
Outputs:
- gamma_three: bfloat16 [256, 512, 2048], P(('occ', 'aux'))
- gamma_two: float32 [2048, 2048], P(('occ', 'aux'))
All inputs are finite; a program needn't handle non-finite values.
Results may differ from a plain program's by a relative error of at most 0.0043.
Values may be sent and summed in bfloat16 or wider, within the bound.
A program may use at most 128 MiB of HBM per device.

v0:
```python
import jax
import jax.numpy as jnp
from jax import lax
from jax.sharding import PartitionSpec as P


def from_behind(shard, axis, by):
    count = lax.axis_size(axis)
    return lax.ppermute(shard, axis, [(i, (i + by) % count) for i in range(count)])


def pair_amplitudes(left_block, right_block, left_energy, right_energy, vir_energy):
    orbitals = left_energy.shape[0]
    virtuals = vir_energy.shape[0]
    ints = lax.dot_general(
        left_block, right_block, (((1,), (1,)), ((), ())), preferred_element_type=jnp.float32
    )
    ints = ints.reshape(orbitals, virtuals, orbitals, virtuals)
    swapped = jnp.transpose(ints, (0, 3, 2, 1))
    gap = (
        vir_energy[None, :, None, None]
        + vir_energy[None, None, None, :]
        - left_energy[:, None, None, None]
        - right_energy[None, None, :, None]
    )
    amps = ((2.0 * ints - swapped) / gap).astype(jnp.bfloat16)
    return amps.reshape(orbitals * virtuals, orbitals * virtuals)


def widen(values):
    return lax.optimization_barrier(values).astype(jnp.float32)


def per_device(occ_energy, vir_energy, factors):
    orbitals, virtuals, panel_width = factors.shape
    width = orbitals * virtuals
    nblocks = lax.axis_size(("occ", "aux"))
    position = lax.axis_index(("occ", "aux"))
    own_flat = factors.reshape(width, panel_width)

    def energies_of(block):
        return lax.dynamic_slice_in_dim(occ_energy, block * orbitals, orbitals)

    own_energy = energies_of(position)
    partner = from_behind(factors, ("occ", "aux"), 1).reshape(width, panel_width)
    partner_energy = energies_of((position - 1) % nblocks)
    amps = pair_amplitudes(own_flat, partner, own_energy, partner_energy, vir_energy)
    gamma_sum = jnp.dot(amps, partner, preferred_element_type=jnp.float32)
    backward = lax.dot_general(
        amps, own_flat, (((0,), (0,)), ((), ())), preferred_element_type=jnp.float32
    ).astype(jnp.bfloat16)
    arrived = from_behind(backward, ("occ", "aux"), -1)
    gamma_sum = gamma_sum + widen(arrived)
    gamma_three = gamma_sum.astype(jnp.bfloat16)
    scale = float(orbitals * nblocks * virtuals) ** (-0.5)
    product = lax.dot_general(
        gamma_three, own_flat, (((0,), (0,)), ((), ())), preferred_element_type=jnp.float32
    )
    gamma_two = lax.psum_scatter(product * scale, ("occ", "aux"), scatter_dimension=0, tiled=True)
    return (gamma_three.reshape(orbitals, virtuals, panel_width), gamma_two)


def solution(mesh):
    placed = (P(), P(), P(("occ", "aux"), None, None))
    return jax.shard_map(
        per_device,
        mesh=mesh,
        in_specs=placed,
        out_specs=(P(("occ", "aux"), None, None), P(("occ", "aux"), None)),
        check_vma=False,
    )
```

profile of v0, /device:TPU:1, one launch (start us, length us, event | category | flops | bytes accessed | tf_op | source)
XLA Modules:
  0.0 928.4 jit_solution(12335244590322857166)
XLA Ops:
  7.2 0.0 reduce-scatter.2.cloned.1.call-start
  7.2 4.5 collective-permute-start
  11.7 0.0 copy-start
  11.7 0.9 fusion.5
  12.6 1.0 broadcast_add_fusion
  13.7 0.3 broadcast_subtract_fusion
  14.0 89.7 %collective-permute-done = bf16[2,512,2048]{2,1,0:T(8,128)(2,1)} collective-permute-done((bf16[2,512,2048]{2,1,0:T(8,128)(2,1)}, bf16[2,512,2048]{2,1,0:T(8,128)(2,1)}, u32[]{:S(2)}, u32[]{:S(2)}) %collective-permute-start) | collective-permute-done | bytes 4194336 | tf_op jit(solution)/shard_map/ppermute | solution.py:9
  103.7 0.0 copy-done
  103.7 8.2 fusion
  112.0 5.3 copy.6
  117.2 6.2 fusion.3
  123.5 4.8 copy.7
  128.3 0.0 copy-start.1
  128.3 0.6 copy.9
  128.9 1.6 copy-done.1
  130.5 4.9 convolution_convert_fusion
  135.4 2.9 collective-permute-start.1
  138.3 91.4 %collective-permute-done.1 = bf16[1024,2048]{1,0:T(8,128)(2,1)S(1)} collective-permute-done((bf16[1024,2048]{1,0:T(8,128)(2,1)S(1)}, bf16[1024,2048]{1,0:T(8,128)(2,1)S(1)}, u32[]{:S(2)}, u32[]{:S(2)}) %collective-permute-start.1) | collective-permute-done | bytes 4194336 | tf_op jit(solution)/shard_map/ppermute | solution.py:9
  229.7 7.0 add_convert_fusion
  236.7 0.0 copy-start.2
  236.7 2.0 copy-done.2
  238.8 11.8 %convolution_multiply_fusion = f32[2048,2048]{1,0:T(8,128)} fusion(bf16[1024,2048]{1,0:T(8,128)(2,1)S(1)} %add_convert_fusion, bf16[1024,2048]{1,0:T(8,128)(2,1)S(1)} %bitcast.30), kind=kOutput, calls=%fused_computation | convolution fusion | flops 8594128896 | bytes 25165824 | tf_op jit(solution)/shard_map/dot_general | solution.py:56
  250.6 0.0 reduce-scatter.2.cloned.1.call-update
  250.6 671.0 %reduce-scatter.2.cloned.1.call-done = f32[16,2048]{1,0:T(8,128)} async-done(((f32[2048,2048]{1,0:T(8,128)}), f32[16,2048]{1,0:T(8,128)}) %reduce-scatter.2.cloned.1.call-update) | async-done | bytes 131088 | tf_op jit(solution)/shard_map/reduce_scatter | solution.py:59
Async XLA Ops:
  7.2 914.4 %reduce-scatter.2.cloned.1.call-start = ((), (), s32[]{:S(2)}) async-start(), calls=%async_computation.1 | async-start | bytes 16908288 | tf_op jit(solution)/shard_map/reduce_scatter | solution.py:59
  7.2 96.5 %collective-permute-start = (bf16[2,512,2048]{2,1,0:T(8,128)(2,1)}, bf16[2,512,2048]{2,1,0:T(8,128)(2,1)}, u32[]{:S(2)}, u32[]{:S(2)}) collective-permute-start(bf16[2,512,2048]{2,1,0:T(8,128)(2,1)} %param.5), channel_id=1, source_target_pairs={{0,1},{1,2},{2,3},{3,4},{4,5},{5,6},{6,7},{7,8},{8,9},{9,10},{10,1... | collective-permute-start | bytes 12582920 | tf_op jit(solution)/shard_map/ppermute | solution.py:9
  11.7 92.0 %copy-start = (bf16[2,512,2048]{2,1,0:T(8,128)(2,1)S(1)}, bf16[2,512,2048]{2,1,0:T(8,128)(2,1)}, u32[]{:S(2)}) copy-start(bf16[2,512,2048]{2,1,0:T(8,128)(2,1)} %param.5) | copy-start | bytes 12582916
  128.3 2.2 copy-start.1
  135.4 94.4 %collective-permute-start.1 = (bf16[1024,2048]{1,0:T(8,128)(2,1)S(1)}, bf16[1024,2048]{1,0:T(8,128)(2,1)S(1)}, u32[]{:S(2)}, u32[]{:S(2)}) collective-permute-start(bf16[1024,2048]{1,0:T(8,128)(2,1)S(1)} %convolution_convert_fusion), channel_id=1, source_target_pairs={{0,127},{1,0},{2,1},{3,2},{4,3},{5,4},{6,5},{7,6},{8,7},{9,8},{10,... | collective-permute-start | bytes 12582920 | tf_op jit(solution)/shard_map/ppermute | solution.py:9
  236.7 2.0 copy-start.2
Sparse Core Ops, SparseCore 0:
  250.7 670.8 reduce-scatter.1
where the time goes:
time: 931 us; the launch traced here: 928 us
  waiting for transfers between devices  852 us (92%)
  matrix products  31.9 us (3%)
  local copies, waits for them, and re-layouts  15.2 us (2%)
  between operations  14.1 us (2%)
    reduce_scatter x1, waiting for transfers between devices, per_device(): lax.psum_scatter(product * scale, ('occ', 'aux'), scatter_dimension=0, ti...  671 us
    ppermute x2, waiting for transfers between devices, from_behind(): lax.ppermute(shard, axis, [(i, (i + by) % count) for i in range(count)])  181 us
  transfers between devices with their start and end apart: 3, of which 3 were waited for; matrix products, arithmetic and copies ran while one was open for 0% of the time, Pallas kernels for 0%

commit v1 on v0

v1 whole, which is shorter than its diff:
```python
import jax
import jax.numpy as jnp
from jax import lax
from jax.experimental import pallas as pl
from jax.experimental.pallas import tpu as pltpu
from jax.sharding import PartitionSpec as P

MESH = pl.DeviceIdType.MESH
NT = (((1,), (1,)), ((), ()))
CHUNKS = 16
TILE = 256


def device(position):
    return (position // 2, position % 2)


def pair_kernel(
    occ, vir, factors, gamma, own, near, far, ints, amps, near_term, far_term, base,
    load_sem, near_send, near_recv, far_send, far_recv,
):
    width, panel = own.shape
    virtuals = vir.shape[1]
    chunk = width // CHUNKS
    count = 2 * lax.axis_size("occ")
    me = lax.axis_index("occ") * 2 + lax.axis_index("aux")
    even = me % 2 == 0
    step = 1 - 2 * (me % 2)
    near_block = (me + step + count) % count
    far_block = (me - step + count) % count
    onward = (me + 2 * step + count) % count
    behind = (me - 2 * step + count) % count

    load = pltpu.make_async_copy(factors, own, load_sem)
    load.start()

    barrier = pltpu.get_barrier_semaphore()
    for other in (near_block, onward, behind):
        pl.semaphore_signal(barrier, inc=1, device_id=device(other), device_id_type=MESH)
    pl.semaphore_wait(barrier, 3)

    def rows(c):
        return pl.ds(c * chunk, chunk)

    direct = [
        pltpu.make_async_remote_copy(
            src_ref=factors.at[rows(c)], dst_ref=near.at[rows(c)],
            send_sem=near_send.at[c], recv_sem=near_recv.at[c],
            device_id=device(near_block), device_id_type=MESH)
        for c in range(CHUNKS)
    ]
    passed = [
        pltpu.make_async_remote_copy(
            src_ref=near.at[rows(c)], dst_ref=far.at[rows(c)],
            send_sem=far_send.at[c], recv_sem=far_recv.at[c],
            device_id=device(onward), device_id_type=MESH)
        for c in range(CHUNKS)
    ]
    for copy in direct:
        copy.start()

    row = jnp.broadcast_to(vir[...], (virtuals, virtuals))
    base[...] = row + row.T
    load.wait()

    def pair_ints(block, which, piece):
        half = piece % 2

        @pl.loop(0, width // TILE)
        def _(r):
            at = pl.ds(pl.multiple_of(r * TILE, TILE), TILE)
            ints[which, at, half * TILE:(half + 1) * TILE] = lax.dot_general(
                own[at, :], block[piece * TILE:(piece + 1) * TILE, :], NT,
                preferred_element_type=jnp.float32)

    def pair_amps(which, other, n):
        other_energy = occ[2 * other + n]
        for i in range(2):
            energy = occ[2 * me + i]
            for a in range(virtuals // TILE):
                for b in range(virtuals // TILE):
                    top, side = i * virtuals + a * TILE, i * virtuals + b * TILE
                    here = ints[which, top:top + TILE, b * TILE:(b + 1) * TILE]
                    swapped = ints[which, side:side + TILE, a * TILE:(a + 1) * TILE].T
                    gap = base[a * TILE:(a + 1) * TILE, b * TILE:(b + 1) * TILE] - energy - other_energy
                    amps[top:top + TILE, b * TILE:(b + 1) * TILE] = (
                        (2.0 * here - swapped) / gap).astype(jnp.bfloat16)

    def pair_term(block, term, n):
        span = 512

        @pl.loop(0, width // TILE)
        def _(r):
            at = pl.ds(pl.multiple_of(r * TILE, TILE), TILE)
            for c in range(panel // span):
                cols = slice(c * span, (c + 1) * span)
                value = jnp.dot(
                    amps[at, :], block[n * virtuals:(n + 1) * virtuals, cols],
                    preferred_element_type=jnp.float32)
                if n == 0:
                    term[at, cols] = value
                else:
                    term[at, cols] += value

    per_piece = TILE // chunk

    def work(block, which, other, term, piece):
        pair_ints(block, which, piece)
        if piece % 2 == 1:
            pair_amps(which, other, piece // 2)
            pair_term(block, term, piece // 2)

    for c in range(CHUNKS):
        direct[c].wait_recv()
        passed[c].start()
        if c >= 1:
            passed[c - 1].wait_recv()
            if c % per_piece == 0:
                work(far, 1, far_block, far_term, c // per_piece - 1)
        if (c + 1) % per_piece == 0:
            work(near, 0, near_block, near_term, c // per_piece)
    passed[CHUNKS - 1].wait_recv()
    work(far, 1, far_block, far_term, 3)

    @pl.loop(0, width // 64)
    def _(r):
        at = pl.ds(pl.multiple_of(r * 64, 64), 64)
        one, two = near_term[at, :], far_term[at, :]
        partner = jnp.where(even, one, two).astype(jnp.bfloat16).astype(jnp.float32)
        gamma[at, :] = (jnp.where(even, two, one) + partner).astype(jnp.bfloat16)

    for c in range(CHUNKS):
        direct[c].wait_send()
        passed[c].wait_send()


def pair_call(occ_energy, vir_energy, flat):
    width, panel = flat.shape
    virtuals = vir_energy.shape[0]
    block = pltpu.VMEM((width, panel), jnp.bfloat16)
    term = pltpu.VMEM((width, panel), jnp.float32)
    return pl.pallas_call(
        pair_kernel,
        out_shape=jax.ShapeDtypeStruct((width, panel), jnp.bfloat16),
        in_specs=[
            pl.BlockSpec(memory_space=pltpu.SMEM),
            pl.BlockSpec(memory_space=pltpu.VMEM),
            pl.BlockSpec(memory_space=pl.ANY),
        ],
        out_specs=pl.BlockSpec(memory_space=pltpu.VMEM),
        scratch_shapes=[
            block, block, block,
            pltpu.VMEM((2, width, virtuals), jnp.float32),
            pltpu.VMEM((width, virtuals), jnp.bfloat16),
            term, term,
            pltpu.VMEM((virtuals, virtuals), jnp.float32),
            pltpu.SemaphoreType.DMA,
        ] + [pltpu.SemaphoreType.DMA((CHUNKS,))] * 4,
        compiler_params=pltpu.CompilerParams(
            collective_id=0, has_side_effects=True, vmem_limit_bytes=60 * 2**20),
        name="pairs",
    )(occ_energy, vir_energy.reshape(1, virtuals), flat)


def per_device(occ_energy, vir_energy, factors):
    orbitals, virtuals, panel = factors.shape
    width = orbitals * virtuals
    nblocks = lax.axis_size(("occ", "aux"))
    flat = factors.reshape(width, panel)
    gamma_three = pair_call(occ_energy, vir_energy, flat)
    scale = float(orbitals * nblocks * virtuals) ** (-0.5)
    product = lax.dot_general(
        gamma_three, flat, (((0,), (0,)), ((), ())), preferred_element_type=jnp.float32)
    gamma_two = lax.psum_scatter(product * scale, ("occ", "aux"), scatter_dimension=0, tiled=True)
    return gamma_three.reshape(orbitals, virtuals, panel), gamma_two


def solution(mesh):
    placed = (P(), P(), P(("occ", "aux"), None, None))
    return jax.shard_map(
        per_device,
        mesh=mesh,
        in_specs=placed,
        out_specs=(P(("occ", "aux"), None, None), P(("occ", "aux"), None)),
        check_vma=False,
    )
```

time: 931 us -> 861 us (0.925)
  waiting for transfers between devices: 852 us -> 686 us
  Pallas kernels: 0 us -> 139 us
  matrix products: 31.9 us -> 15.3 us
  local copies, waits for them, and re-layouts: 15.2 us -> 4.79 us
    ppermute x2 -> x0, waiting for transfers between devices: 181 us -> none  [from_behind(): lax.ppermute(shard, axis, [(i, (i + by) % count) for i in range(count)])]
    pallas_call x0 -> x1, Pallas kernels: none -> 139 us  [pair_call(): pl.pallas_call(pair_kernel, out_shape=jax.ShapeDtypeStruct((width, panel)...]
    dot_general x4 -> x1, matrix products: 31.9 us -> 15.3 us  [per_device(): lax.dot_general(gamma_three, flat, (((0,), (0,)), ((), ())), preferred_el...]
    reduce_scatter x1, waiting for transfers between devices: 671 us -> 686 us  [per_device(): lax.psum_scatter(product * scale, ('occ', 'aux'), scatter_dimension=0, ti...]
  transfers between devices with their start and end apart: 3 -> 1, of which waited for: 3 -> 1; matrix products, arithmetic and copies ran while one was open for 0% -> 0% of each run, Pallas kernels for 0% -> 0%
where the time goes in v1:
time: 861 us; the launch traced here: 859 us
  waiting for transfers between devices  686 us (80%)
  Pallas kernels  139 us (16%)
  matrix products  15.3 us (2%)
  between operations  14 us (2%)
    reduce_scatter x1, waiting for transfers between devices, per_device(): lax.psum_scatter(product * scale, ('occ', 'aux'), scatter_dimension=0, ti...  686 us
    pallas_call x1, Pallas kernels, pair_call(): pl.pallas_call(pair_kernel, out_shape=jax.ShapeDtypeStruct((width, panel)...  139 us
  transfers between devices with their start and end apart: 1, of which 1 were waited for; matrix products, arithmetic and copies ran while one was open for 0% of the time, Pallas kernels for 0%

profile of v1, /device:TPU:1, one launch (start us, length us, event | category | flops | bytes accessed | tf_op | source)
XLA Modules:
  0.0 859.3 jit_solution(10050255301744979170)
XLA Ops:
  7.2 0.0 reduce-scatter.2.cloned.1.call-start
  7.2 139.4 %pairs.1 = bf16[1024,2048]{1,0:T(8,128)(2,1)} custom-call(f32[256]{0:T(256)} %occ.1, f32[1,512]{1,0:T(1,128)} %bitcast.8, bf16[1024,2048]{1,0:T(8,128)(2,1)} %bitcast.6), custom_call_target="tpu_custom_call" | custom-call | tf_op jit(solution)/shard_map/pairs/pallas_call | solution.py:142
  146.6 15.3 %convolution_multiply_fusion = f32[2048,2048]{1,0:T(8,128)} fusion(bf16[1024,2048]{1,0:T(8,128)(2,1)} %pairs.1, bf16[1024,2048]{1,0:T(8,128)(2,1)} %bitcast.7), kind=kOutput, calls=%fused_computation | convolution fusion | flops 8594128896 | bytes 25165824 | tf_op jit(solution)/shard_map/dot_general | solution.py:172
  162.0 0.0 reduce-scatter.2.cloned.1.call-update
  162.0 685.7 %reduce-scatter.2.cloned.1.call-done = f32[16,2048]{1,0:T(8,128)} async-done(((f32[2048,2048]{1,0:T(8,128)}), f32[16,2048]{1,0:T(8,128)}) %reduce-scatter.2.cloned.1.call-update) | async-done | bytes 131088 | tf_op jit(solution)/shard_map/reduce_scatter | solution.py:174
  847.6 4.8 copy.6
Async XLA Ops:
  7.2 840.5 %reduce-scatter.2.cloned.1.call-start = ((), (), s32[]{:S(2)}) async-start(), calls=%async_computation.1 | async-start | bytes 16908288 | tf_op jit(solution)/shard_map/reduce_scatter | solution.py:174
Sparse Core Ops, SparseCore 0:
  162.1 685.5 reduce-scatter.1

commit v2 on v1

--- a/solution.py
+++ b/solution.py
@@ -162,16 +162,259 @@
     )(occ_energy, vir_energy.reshape(1, virtuals), flat)
 
 
+TN = (((0,), (0,)), ((), ()))
+COLS = ((0, 384), (384, 384), (768, 256))
+NEAR_FIRST = (2, 1, 3, 0)
+
+
+def coordinates():
+    occ, aux = lax.axis_index("occ"), lax.axis_index("aux")
+    return (occ // 8) % 4, (occ // 2) % 4, aux * 2 + occ // 32, occ % 2
+
+
+def chip(x, y, z, core):
+    return ((z % 2) * 32 + x * 8 + y * 2 + core, z // 2)
+
+
+def sum_kernel(
+    gamma_hbm, factors, out, gamma, own, outgoing, incoming, held, part,
+    first0, first1, first2, mid0, mid1, mid2, second0, second1, second2,
+    late0, late1, late2, third0, third1, third2, rows, rows_in,
+    load_sem, core_send, core_recv, send1, recv1, send2, recv2, send3, recv3, end_send, end_recv,
+):
+    x, y, z, core = coordinates()
+    z_lo, z_hi = z % 2, z // 2
+    half = out.shape[1] // 2
+    mine = pl.multiple_of(core * half, half)
+    others = pl.multiple_of((1 - core) * half, half)
+    scale = float(128 * gamma.shape[0]) ** (-0.5)
+
+    def along(axis, by):
+        place = [x, y, z]
+        place[axis] = (place[axis] + by) % 4
+        return chip(*place, core)
+
+    load_a = pltpu.make_async_copy(gamma_hbm, gamma, load_sem.at[0])
+    load_b = pltpu.make_async_copy(factors, own, load_sem.at[1])
+    load_a.start()
+    load_b.start()
+    barrier = pltpu.get_barrier_semaphore()
+    for axis in range(3):
+        for by in (1, 2, 3):
+            pl.semaphore_signal(barrier, inc=1, device_id=along(axis, by), device_id_type=MESH)
+    pl.semaphore_signal(barrier, inc=1, device_id=chip(x, y, z, 1 - core), device_id_type=MESH)
+    pl.semaphore_wait(barrier, 10)
+    load_a.wait()
+    load_b.wait()
+
+    def remote(src, dst, send, recv, target):
+        return pltpu.make_async_remote_copy(
+            src_ref=src, dst_ref=dst, send_sem=send, recv_sem=recv,
+            device_id=target, device_id_type=MESH)
+
+    tiles = [(e, d) for d in NEAR_FIRST for e in (1, 0)]
+    swaps = []
+    waits = [[], [], []]
+
+    def finish(t):
+        e, d = tiles[t]
+        zl, xt = (z_lo + e) % 2, (x + d) % 4
+        swaps[t].wait_recv()
+        for yy in range(4):
+            for c in range(2):
+                for zh in range(2):
+                    at = ((yy * 2 + c) * 2 + zh) * 16
+                    total = held[t % 2, at:at + 16, :] + incoming[t, at:at + 16, :].astype(jnp.float32)
+                    part[zl, xt, yy, zh, c * 16:(c + 1) * 16, :] = total.astype(jnp.bfloat16)
+        copies = []
+        if d:
+            cols = pl.ds(*COLS[0])
+            copies.append((0, part.at[zl, xt, :, :, :, cols], first0.at[d - 1, zl], along(0, d)))
+        for by in (2, 1, 3):
+            cols = pl.ds(*COLS[1])
+            copies.append((1, part.at[zl, xt, (y + by) % 4, :, :, cols], first1.at[by - 1, zl, xt], along(1, by)))
+        for by in ((1, 3) if e else (2,)):
+            cols = pl.ds(*COLS[2])
+            copies.append((2, part.at[zl, xt, :, ((z + by) % 4) // 2, :, cols], first2.at[by - 1, xt], along(2, by)))
+        for k, src, dst, target in copies:
+            n = sum(len(w) for w in waits)
+            copy = remote(src, dst, send1.at[n], recv1.at[n], target)
+            copy.start()
+            waits[k].append(copy)
+
+    for t, (e, d) in enumerate(tiles):
+        zl, xt = (z_lo + e) % 2, (x + d) % 4
+        at = pl.ds(pl.multiple_of((zl * 4 + xt) * 256, 256), 256)
+        left = gamma[:, at]
+        for c in range(2):
+            cols = pl.ds(pl.multiple_of(others + c * 512, 512), 512)
+            outgoing[t, :, c * 512:(c + 1) * 512] = (lax.dot_general(
+                left, own[:, cols], TN, preferred_element_type=jnp.float32) * scale).astype(jnp.bfloat16)
+        swap = remote(outgoing.at[t], incoming.at[t], core_send.at[t], core_recv.at[t], chip(x, y, z, 1 - core))
+        swap.start()
+        swaps.append(swap)
+        for c in range(2):
+            cols = pl.ds(pl.multiple_of(mine + c * 512, 512), 512)
+            held[t % 2, :, c * 512:(c + 1) * 512] = lax.dot_general(
+                left, own[:, cols], TN, preferred_element_type=jnp.float32) * scale
+        if t:
+            finish(t - 1)
+    finish(len(tiles) - 1)
+
+    def wide(value):
+        return value.astype(jnp.float32)
+
+    seconds = [[], [], []]
+
+    def second(k, by, src, dst, axis):
+        n = k * 3 + by - 1
+        copy = remote(src, dst, send2.at[n], recv2.at[n], along(axis, by))
+        copy.start()
+        seconds[k].append(copy)
+
+    for copy in waits[2]:
+        copy.wait_recv()
+    for xx in range(4):
+        for yy in range(4):
+            total = wide(part[z_lo, xx, yy, z_hi, :, 768:1024])
+            for j in range(3):
+                total += wide(first2[j, xx, yy])
+            mid2[xx, yy] = total.astype(mid2.dtype)
+    for by in (2, 1, 3):
+        second(2, by, mid2.at[(x + by) % 4], second2.at[by - 1], 0)
+
+    for copy in waits[0]:
+        copy.wait_recv()
+    for zl in range(2):
+        for yy in range(4):
+            for zh in range(2):
+                total = wide(part[zl, x, yy, zh, :, 0:384])
+                for j in range(3):
+                    total += wide(first0[j, zl, yy, zh])
+                mid0[yy, zl, zh] = total.astype(mid0.dtype)
+    for by in (2, 1, 3):
+        second(0, by, mid0.at[(y + by) % 4], second0.at[by - 1], 1)
+
+    for copy in waits[1]:
+        copy.wait_recv()
+    for zl in range(2):
+        for xx in range(4):
+            for zh in range(2):
+                total = wide(part[zl, xx, y, zh, :, 384:768])
+                for j in range(3):
+                    total += wide(first1[j, zl, xx, zh])
+                mid1[zl, zh, xx] = total.astype(mid1.dtype)
+    for by in (2, 1, 3):
+        far = (z + by) % 4
+        second(1, by, mid1.at[far % 2, far // 2], second1.at[by - 1], 2)
+
+    thirds = [[], [], []]
+
+    def third(k, by, src, dst, axis):
+        n = k * 3 + by - 1
+        copy = remote(src, dst, send3.at[n], recv3.at[n], along(axis, by))
+        copy.start()
+        thirds[k].append(copy)
+
+    for copy in seconds[2]:
+        copy.wait_recv()
+    for yy in range(4):
+        total = wide(mid2[x, yy])
+        for j in range(3):
+            total += wide(second2[j, yy])
+        late2[yy] = total
+    for by in (2, 1, 3):
+        third(2, by, late2.at[(y + by) % 4], third2.at[by - 1], 1)
+
+    for copy in seconds[0]:
+        copy.wait_recv()
+    for zl in range(2):
+        for zh in range(2):
+            total = wide(mid0[y, zl, zh])
+            for j in range(3):
+                total += wide(second0[j, zl, zh])
+            late0[zl, zh] = total
+    for by in (2, 1, 3):
+        far = (z + by) % 4
+        third(0, by, late0.at[far % 2, far // 2], third0.at[by - 1], 2)
+
+    for copy in seconds[1]:
+        copy.wait_recv()
+    for xx in range(4):
+        total = wide(mid1[z_lo, z_hi, xx])
+        for j in range(3):
+            total += wide(second1[j, xx])
+        late1[xx] = total
+    for by in (2, 1, 3):
+        third(1, by, late1.at[(x + by) % 4], third1.at[by - 1], 0)
+
+    for k in (2, 0, 1):
+        for copy in thirds[k]:
+            copy.wait_recv()
+    rows[:, 0:384] = late0[z_lo, z_hi] + third0[0] + third0[1] + third0[2]
+    rows[:, 384:768] = late1[x] + third1[0] + third1[1] + third1[2]
+    rows[:, 768:1024] = late2[y] + third2[0] + third2[1] + third2[2]
+    last = remote(
+        rows.at[pl.ds(pl.multiple_of((1 - core) * 16, 16), 16)], rows_in, end_send, end_recv,
+        chip(x, y, z, 1 - core))
+    last.start()
+    out[:, pl.ds(mine, half)] = rows[pl.ds(pl.multiple_of(core * 16, 16), 16), :]
+    last.wait_recv()
+    out[:, pl.ds(others, half)] = rows_in[...]
+
+    for copy in swaps + waits[0] + waits[1] + waits[2] + sum(seconds, []) + sum(thirds, []) + [last]:
+        copy.wait_send()
+
+
+def sum_call(gamma, flat):
+    width, panel = flat.shape
+    half = panel // 2
+    low, full = jnp.bfloat16, jnp.float32
+    dma = pltpu.SemaphoreType.DMA
+    return pl.pallas_call(
+        sum_kernel,
+        out_shape=jax.ShapeDtypeStruct((16, panel), jnp.float32),
+        in_specs=[pl.BlockSpec(memory_space=pl.ANY)] * 2,
+        out_specs=pl.BlockSpec(memory_space=pltpu.VMEM),
+        scratch_shapes=[
+            pltpu.VMEM((width, panel), low),
+            pltpu.VMEM((width, panel), low),
+            pltpu.VMEM((8, 256, half), low),
+            pltpu.VMEM((8, 256, half), low),
+            pltpu.VMEM((2, 256, half), full),
+            pltpu.VMEM((2, 4, 4, 2, 32, half), low),
+            pltpu.VMEM((3, 2, 4, 2, 32, 384), low),
+            pltpu.VMEM((3, 2, 4, 2, 32, 384), low),
+            pltpu.VMEM((3, 4, 4, 32, 256), low),
+            pltpu.VMEM((4, 2, 2, 32, 384), low),
+            pltpu.VMEM((2, 2, 4, 32, 384), low),
+            pltpu.VMEM((4, 4, 32, 256), low),
+            pltpu.VMEM((3, 2, 2, 32, 384), low),
+            pltpu.VMEM((3, 4, 32, 384), low),
+            pltpu.VMEM((3, 4, 32, 256), low),
+            pltpu.VMEM((2, 2, 32, 384), full),
+            pltpu.VMEM((4, 32, 384), full),
+            pltpu.VMEM((4, 32, 256), full),
+            pltpu.VMEM((3, 32, 384), full),
+            pltpu.VMEM((3, 32, 384), full),
+            pltpu.VMEM((3, 32, 256), full),
+            pltpu.VMEM((32, half), full),
+            pltpu.VMEM((16, half), full),
+            dma((2,)), dma((8,)), dma((8,)), dma((42,)), dma((42,)),
+            dma((9,)), dma((9,)), dma((9,)), dma((9,)), dma, dma,
+        ],
+        compiler_params=pltpu.CompilerParams(
+            collective_id=1, has_side_effects=True, vmem_limit_bytes=60 * 2**20),
+        name="sums",
+    )(gamma, flat)
+
+
 def per_device(occ_energy, vir_energy, factors):
     orbitals, virtuals, panel = factors.shape
     width = orbitals * virtuals
-    nblocks = lax.axis_size(("occ", "aux"))
     flat = factors.reshape(width, panel)
     gamma_three = pair_call(occ_energy, vir_energy, flat)
-    scale = float(orbitals * nblocks * virtuals) ** (-0.5)
-    product = lax.dot_general(
-        gamma_three, flat, (((0,), (0,)), ((), ())), preferred_element_type=jnp.float32)
-    gamma_two = lax.psum_scatter(product * scale, ("occ", "aux"), scatter_dimension=0, tiled=True)
+    gamma_two = sum_call(gamma_three, flat)
     return gamma_three.reshape(orbitals, virtuals, panel), gamma_two
 
 

time: 861 us -> 204 us (0.24)
  waiting for transfers between devices: 686 us -> 0 us
  Pallas kernels: 139 us -> 198 us
  matrix products: 15.3 us -> 0 us
  between operations: 14 us -> 0.65 us
    reduce_scatter x1 -> x0, waiting for transfers between devices: 686 us -> none  [per_device(): lax.psum_scatter(product * scale, ('occ', 'aux'), scatter_dimension=0, ti...]
    pallas_call x0 -> x1, Pallas kernels: none -> 58.4 us  [sum_call(): pl.pallas_call(sum_kernel, out_shape=jax.ShapeDtypeStruct((16, panel), jn...]
    dot_general x1 -> x0, matrix products: 15.3 us -> none  [per_device(): lax.dot_general(gamma_three, flat, (((0,), (0,)), ((), ())), preferred_el...]
  transfers between devices with their start and end apart: 1 -> 0, of which waited for: 1 -> 0; matrix products, arithmetic and copies ran while one was open for 0% -> 0% of each run, Pallas kernels for 0% -> 0%
where the time goes in v2:
time: 204 us
  Pallas kernels  198 us (97%)
  local copies, waits for them, and re-layouts  5.48 us (3%)
    pallas_call x1, Pallas kernels, pair_call(): pl.pallas_call(pair_kernel, out_shape=jax.ShapeDtypeStruct((width, panel)...  140 us
    pallas_call x1, Pallas kernels, sum_call(): pl.pallas_call(sum_kernel, out_shape=jax.ShapeDtypeStruct((16, panel), jn...  58.4 us
    unnamed x4, local copies, waits for them, and re-layouts  5.48 us

profile of v2, /device:TPU:1, one launch (start us, length us, event | category | flops | bytes accessed | tf_op | source)
XLA Modules:
  0.0 204.1 jit_solution(1872160420659097166)
XLA Ops:
  0.6 139.6 %pairs.1.gamma_hbm = bf16[1024,2048]{1,0:T(8,128)(2,1)} custom-call(f32[256]{0:T(256)} %occ.1, f32[1,512]{1,0:T(1,128)} %bitcast.6, bf16[1024,2048]{1,0:T(8,128)(2,1)} %bitcast.4), custom_call_target="tpu_custom_call" | custom-call | tf_op jit(solution)/shard_map/pairs/pallas_call | solution.py:142
  140.2 58.4 %sums.1 = f32[16,2048]{1,0:T(8,128)} custom-call(bf16[1024,2048]{1,0:T(8,128)(2,1)} %pairs.1.gamma_hbm, bf16[1024,2048]{1,0:T(8,128)(2,1)} %bitcast.5), custom_call_target="tpu_custom_call" | custom-call | tf_op jit(solution)/shard_map/sums/pallas_call | solution.py:374
  198.6 0.0 copy-start
  198.6 4.8 %copy.7 = bf16[2,512,2048]{2,1,0:T(8,128)(2,1)} copy(bf16[2,512,2048]{2,1,0:T(8,128)(2,1)} %bitcast.3) | data formatting | bytes 8388608
  203.5 0.0 copy-done
  203.5 0.7 copy.8
Async XLA Ops:
  198.6 4.8 %copy-start = (f32[16,2048]{1,0:T(8,128)S(1)}, f32[16,2048]{1,0:T(8,128)}, u32[]{:S(2)}) copy-start(f32[16,2048]{1,0:T(8,128)} %sums.1) | copy-start | bytes 393220

commit v3 on v2

v3 whole, which is shorter than its diff:
```python
import jax
import jax.numpy as jnp
from jax import lax
from jax.experimental import pallas as pl
from jax.experimental.pallas import tpu as pltpu
from jax.sharding import PartitionSpec as P

MESH = pl.DeviceIdType.MESH
NT = (((1,), (1,)), ((), ()))
TN = (((0,), (0,)), ((), ()))
CHUNKS = 16
LAG = 3
TILE = 256
COLS = ((0, 384), (384, 384), (768, 256))
NEAR_FIRST = (2, 1, 3, 0)
SLOTS = 4


def device(position):
    return (position // 2, position % 2)


def by_plane(z, values):
    return jnp.where(z == 0, values[0], jnp.where(z == 1, values[1], jnp.where(z == 2, values[2], values[3])))


def coordinates():
    occ, aux = lax.axis_index("occ"), lax.axis_index("aux")
    return (occ // 8) % 4, (occ // 2) % 4, aux * 2 + occ // 32, occ % 2


def chip(x, y, z, core):
    return ((z % 2) * 32 + x * 8 + y * 2 + core, z // 2)


def density_kernel(
    occ, vir, factors, gamma_out, out, own, near, far, ints, amps, near_term, far_term, base, transit,
    gamma, outgoing, incoming, part,
    first0, first1, first2, mid0, mid1, mid2, second0, second1, second2,
    late0, late1, late2, third0, third1, third2, rows, rows_in,
    load_sem, near_send, near_recv, far_send, far_recv, transit_send, transit_recv,
    store_sem, core_send, core_recv, send1, recv1, send2, recv2, send3, recv3, end_send, end_recv,
):
    width, panel = own.shape
    virtuals = vir.shape[1]
    chunk = width // CHUNKS
    count = 2 * lax.axis_size("occ")
    me = lax.axis_index("occ") * 2 + lax.axis_index("aux")
    even = me % 2 == 0
    step = 1 - 2 * (me % 2)
    near_block = (me + step + count) % count
    far_block = (me - step + count) % count
    onward = (me + 2 * step + count) % count
    behind = (me - 2 * step + count) % count

    x, y, z, core = coordinates()
    column = jnp.where(z < 2, x * 4 + y, 15 - (x * 4 + y))
    crosses = me % 64 == jnp.where(even, 62, 1)
    crossed = (me % 64 == 0) | (me % 64 == 63)
    relays = core == jnp.where(z < 2, 1, 0)
    relay_from = by_plane(z, (126, 62, 65, 1))
    relay_to = by_plane(z, (0, 64, 63, 127))

    def relay_of(c, plane):
        at = jnp.where(plane < 2, c * 2 + 1, (CHUNKS - 1 - c) * 2)
        return ((plane % 2) * 32 + at, plane // 2)

    plane_on = by_plane(z, (1, 0, 3, 2))

    z_lo, z_hi = z % 2, z // 2
    half = panel // 2
    mine = pl.multiple_of(core * half, half)
    others = pl.multiple_of((1 - core) * half, half)
    scale = float(count * width) ** (-0.5)

    def along(axis, by):
        place = [x, y, z]
        place[axis] = (place[axis] + by) % 4
        return chip(*place, core)

    def remote(src, dst, send, recv, target):
        return pltpu.make_async_remote_copy(
            src_ref=src, dst_ref=dst, send_sem=send, recv_sem=recv,
            device_id=target, device_id_type=MESH)

    load = pltpu.make_async_copy(factors, own, load_sem)
    load.start()

    barrier = pltpu.get_barrier_semaphore()
    for other in (near_block, onward, behind):
        pl.semaphore_signal(barrier, inc=1, device_id=device(other), device_id_type=MESH)
    for axis in range(3):
        for by in (1, 2, 3):
            pl.semaphore_signal(barrier, inc=1, device_id=along(axis, by), device_id_type=MESH)
    pl.semaphore_signal(barrier, inc=1, device_id=chip(x, y, z, 1 - core), device_id_type=MESH)

    @pl.when(crossed)
    def _():
        for c in range(CHUNKS):
            pl.semaphore_signal(barrier, inc=1, device_id=relay_of(c, z), device_id_type=MESH)

    @pl.when(relays)
    def _():
        pl.semaphore_signal(barrier, inc=1, device_id=device(relay_from), device_id_type=MESH)

    pl.semaphore_wait(barrier, 13 + jnp.where(crosses, CHUNKS, 0) + jnp.where(relays, 1, 0))

    def span(c):
        return pl.ds(c * chunk, chunk)

    direct = [
        pltpu.make_async_remote_copy(
            src_ref=factors.at[span(c)], dst_ref=near.at[span(c)],
            send_sem=near_send.at[c], recv_sem=near_recv.at[c],
            device_id=device(near_block), device_id_type=MESH)
        for c in range(CHUNKS)
    ]
    passed = [
        pltpu.make_async_remote_copy(
            src_ref=near.at[span(c)], dst_ref=far.at[span(c)],
            send_sem=far_send.at[c], recv_sem=far_recv.at[c],
            device_id=device(onward), device_id_type=MESH)
        for c in range(CHUNKS)
    ]
    crossing = [
        pltpu.make_async_remote_copy(
            src_ref=near.at[span(c)], dst_ref=transit,
            send_sem=far_send.at[c], recv_sem=transit_recv,
            device_id=relay_of(c, plane_on), device_id_type=MESH)
        for c in range(CHUNKS)
    ]
    relayed = pltpu.make_async_remote_copy(
        src_ref=transit, dst_ref=far.at[pl.ds(pl.multiple_of(column * chunk, chunk), chunk)],
        send_sem=transit_send, recv_sem=far_recv.at[column],
        device_id=device(relay_to), device_id_type=MESH)
    for copy in direct:
        copy.start()

    def pass_on(c):
        pl.when(crosses)(crossing[c].start)
        pl.when(jnp.logical_not(crosses))(passed[c].start)

    def relay(c):
        @pl.when(relays & (column == c))
        def _():
            crossing[c].wait_recv()
            relayed.start()

    row = jnp.broadcast_to(vir[...], (virtuals, virtuals))
    base[...] = row + row.T
    load.wait()

    def pair_ints(block, which, piece):
        left = piece % 2 * TILE

        @pl.loop(0, width // 512)
        def _(r):
            at = pl.ds(pl.multiple_of(r * 512, 512), 512)
            ints[which, at, left:left + TILE] = lax.dot_general(
                own[at, :], block[piece * TILE:(piece + 1) * TILE, :], NT,
                preferred_element_type=jnp.float32)

    def pair_amps(which, other, n):
        other_energy = occ[2 * other + n]
        for i in range(2):
            energy = occ[2 * me + i]
            for a in range(virtuals // TILE):
                for b in range(virtuals // TILE):
                    top, side = i * virtuals + a * TILE, i * virtuals + b * TILE
                    here = ints[which, top:top + TILE, b * TILE:(b + 1) * TILE]
                    swapped = ints[which, side:side + TILE, a * TILE:(a + 1) * TILE].T
                    gap = base[a * TILE:(a + 1) * TILE, b * TILE:(b + 1) * TILE] - energy - other_energy
                    amps[which, top:top + TILE, b * TILE:(b + 1) * TILE] = (
                        (2.0 * here - swapped) / gap).astype(jnp.bfloat16)

    def pair_term(which, block, term):
        @pl.loop(0, width // TILE)
        def _(r):
            at = pl.ds(pl.multiple_of(r * TILE, TILE), TILE)
            for c in range(0, panel, 512):
                term[at, c:c + 512] = jnp.dot(
                    amps[which, at, :], block[0:virtuals, c:c + 512], preferred_element_type=jnp.float32)

    per_piece = TILE // chunk

    def work(block, which, other, term, piece):
        pair_ints(block, which, piece)
        if piece % 2 == 1:
            pair_amps(which, other, piece // 2)
            if piece == 1:
                pair_term(which, block, term)

    for c in range(CHUNKS):
        direct[c].wait_recv()
        pass_on(c)
        if c >= 2:
            relay(c - 2)
        if c >= LAG:
            passed[c - LAG].wait_recv()
            if (c - LAG + 1) % per_piece == 0:
                work(far, 1, far_block, far_term, (c - LAG) // per_piece)
        if (c + 1) % per_piece == 0:
            work(near, 0, near_block, near_term, c // per_piece)
    relay(CHUNKS - 2)
    relay(CHUNKS - 1)
    for c in range(CHUNKS - LAG, CHUNKS):
        passed[c].wait_recv()
    work(far, 1, far_block, far_term, 3)

    tiles = [(e, d) for d in NEAR_FIRST for e in (1, 0)]
    swaps = []
    waits = [[], [], []]

    def finish(t):
        e, d = tiles[t]
        zl, xt = (z_lo + e) % 2, (x + d) % 4
        swaps[t].wait_recv()
        for yy in range(4):
            for c in range(2):
                for zh in range(2):
                    at = ((yy * 2 + c) * 2 + zh) * 16
                    total = jnp.concatenate(
                        [ints[t % 2, at:at + 16, :], ints[t % 2, TILE + at:TILE + at + 16, :]], axis=1)
                    total += incoming[t, at:at + 16, :].astype(jnp.float32)
                    part[zl, xt, yy, zh, c * 16:(c + 1) * 16, :] = total.astype(jnp.bfloat16)
        copies = []
        if d:
            cols = pl.ds(*COLS[0])
            copies.append((0, part.at[zl, xt, :, :, :, cols], first0.at[d - 1, zl], along(0, d)))
        for by in (2, 1, 3):
            cols = pl.ds(*COLS[1])
            copies.append((1, part.at[zl, xt, (y + by) % 4, :, :, cols], first1.at[by - 1, zl, xt], along(1, by)))
        for by in ((1, 3) if e else (2,)):
            cols = pl.ds(*COLS[2])
            copies.append((2, part.at[zl, xt, :, ((z + by) % 4) // 2, :, cols], first2.at[by - 1, xt], along(2, by)))
        for k, src, dst, target in copies:
            n = sum(len(w) for w in waits)
            copy = remote(src, dst, send1.at[n], recv1.at[n], target)
            copy.start()
            waits[k].append(copy)

    stores = []
    for t, (e, d) in enumerate(tiles):
        zl, xt = (z_lo + e) % 2, (x + d) % 4
        at = pl.ds(pl.multiple_of((zl * 4 + xt) * TILE, TILE), TILE)

        @pl.loop(0, width // 512)
        def _(r):
            group = pl.ds(pl.multiple_of(r * 512, 512), 512)
            one = near_term[group, at] + jnp.dot(
                amps[0, group, :], near[virtuals:width, at], preferred_element_type=jnp.float32)
            two = far_term[group, at] + jnp.dot(
                amps[1, group, :], far[virtuals:width, at], preferred_element_type=jnp.float32)
            partner = jnp.where(even, one, two).astype(jnp.bfloat16).astype(jnp.float32)
            gamma[group, at] = (jnp.where(even, two, one) + partner).astype(jnp.bfloat16)

        store = pltpu.make_async_copy(gamma.at[:, at], gamma_out.at[:, at], store_sem.at[t])
        store.start()
        stores.append(store)
        left = gamma[:, at]
        if t >= SLOTS:
            swaps[t - SLOTS].wait_send()
        for c in range(0, half, 512):
            cols = pl.ds(pl.multiple_of(others + c, 512), 512)
            outgoing[t % SLOTS, :, c:c + 512] = (lax.dot_general(
                left, own[:, cols], TN, preferred_element_type=jnp.float32) * scale).astype(jnp.bfloat16)
        swap = remote(
            outgoing.at[t % SLOTS], incoming.at[t], core_send.at[t], core_recv.at[t], chip(x, y, z, 1 - core))
        swap.start()
        swaps.append(swap)
        for c in range(2):
            cols = pl.ds(pl.multiple_of(mine + c * 512, 512), 512)
            ints[t % 2, c * TILE:(c + 1) * TILE, :] = lax.dot_general(
                left, own[:, cols], TN, preferred_element_type=jnp.float32) * scale
        if t:
            finish(t - 1)
    finish(len(tiles) - 1)

    def wide(value):
        return value.astype(jnp.float32)

    seconds = [[], [], []]

    def second(k, by, src, dst, axis):
        n = k * 3 + by - 1
        copy = remote(src, dst, send2.at[n], recv2.at[n], along(axis, by))
        copy.start()
        seconds[k].append(copy)

    for copy in waits[2]:
        copy.wait_recv()
    for xx in range(4):
        for yy in range(4):
            total = wide(part[z_lo, xx, yy, z_hi, :, 768:1024])
            for j in range(3):
                total += wide(first2[j, xx, yy])
            mid2[xx, yy] = total.astype(mid2.dtype)
    for by in (2, 1, 3):
        second(2, by, mid2.at[(x + by) % 4], second2.at[by - 1], 0)

    for copy in waits[0]:
        copy.wait_recv()
    for zl in range(2):
        for yy in range(4):
            for zh in range(2):
                total = wide(part[zl, x, yy, zh, :, 0:384])
                for j in range(3):
                    total += wide(first0[j, zl, yy, zh])
                mid0[yy, zl, zh] = total.astype(mid0.dtype)
    for by in (2, 1, 3):
        second(0, by, mid0.at[(y + by) % 4], second0.at[by - 1], 1)

    for copy in waits[1]:
        copy.wait_recv()
    for zl in range(2):
        for xx in range(4):
            for zh in range(2):
                total = wide(part[zl, xx, y, zh, :, 384:768])
                for j in range(3):
                    total += wide(first1[j, zl, xx, zh])
                mid1[zl, zh, xx] = total.astype(mid1.dtype)
    for by in (2, 1, 3):
        far = (z + by) % 4
        second(1, by, mid1.at[far % 2, far // 2], second1.at[by - 1], 2)

    thirds = [[], [], []]

    def third(k, by, src, dst, axis):
        n = k * 3 + by - 1
        copy = remote(src, dst, send3.at[n], recv3.at[n], along(axis, by))
        copy.start()
        thirds[k].append(copy)

    for copy in seconds[2]:
        copy.wait_recv()
    for yy in range(4):
        total = wide(mid2[x, yy])
        for j in range(3):
            total += wide(second2[j, yy])
        late2[yy] = total
    for by in (2, 1, 3):
        third(2, by, late2.at[(y + by) % 4], third2.at[by - 1], 1)

    for copy in seconds[0]:
        copy.wait_recv()
    for zl in range(2):
        for zh in range(2):
            total = wide(mid0[y, zl, zh])
            for j in range(3):
                total += wide(second0[j, zl, zh])
            late0[zl, zh] = total
    for by in (2, 1, 3):
        far = (z + by) % 4
        third(0, by, late0.at[far % 2, far // 2], third0.at[by - 1], 2)

    for copy in seconds[1]:
        copy.wait_recv()
    for xx in range(4):
        total = wide(mid1[z_lo, z_hi, xx])
        for j in range(3):
            total += wide(second1[j, xx])
        late1[xx] = total
    for by in (2, 1, 3):
        third(1, by, late1.at[(x + by) % 4], third1.at[by - 1], 0)

    for k in (2, 0, 1):
        for copy in thirds[k]:
            copy.wait_recv()
    rows[:, 0:384] = late0[z_lo, z_hi] + third0[0] + third0[1] + third0[2]
    rows[:, 384:768] = late1[x] + third1[0] + third1[1] + third1[2]
    rows[:, 768:1024] = late2[y] + third2[0] + third2[1] + third2[2]
    last = remote(
        rows.at[pl.ds(pl.multiple_of((1 - core) * 16, 16), 16)], rows_in, end_send, end_recv,
        chip(x, y, z, 1 - core))
    last.start()
    out[:, pl.ds(mine, half)] = rows[pl.ds(pl.multiple_of(core * 16, 16), 16), :]
    last.wait_recv()
    out[:, pl.ds(others, half)] = rows_in[...]

    for c in range(CHUNKS):
        direct[c].wait_send()
        passed[c].wait_send()
    pl.when(relays)(relayed.wait_send)
    for store in stores:
        store.wait()
    for copy in swaps[-SLOTS:] + waits[0] + waits[1] + waits[2] + sum(seconds, []) + sum(thirds, []) + [last]:
        copy.wait_send()


def density_call(occ_energy, vir_energy, flat):
    width, panel = flat.shape
    virtuals = vir_energy.shape[0]
    half = panel // 2
    low, full = jnp.bfloat16, jnp.float32
    dma = pltpu.SemaphoreType.DMA
    block = pltpu.VMEM((width, panel), low)
    term = pltpu.VMEM((width, panel), full)
    return pl.pallas_call(
        density_kernel,
        out_shape=(
            jax.ShapeDtypeStruct((width, panel), low),
            jax.ShapeDtypeStruct((16, panel), full),
        ),
        in_specs=[
            pl.BlockSpec(memory_space=pltpu.SMEM),
            pl.BlockSpec(memory_space=pltpu.VMEM),
            pl.BlockSpec(memory_space=pl.ANY),
        ],
        out_specs=(pl.BlockSpec(memory_space=pl.ANY), pl.BlockSpec(memory_space=pltpu.VMEM)),
        scratch_shapes=[
            block, block, block,
            pltpu.VMEM((2, width, virtuals), full),
            pltpu.VMEM((2, width, virtuals), low),
            term, term,
            pltpu.VMEM((virtuals, virtuals), full),
            pltpu.VMEM((width // CHUNKS, panel), low),
            block,
            pltpu.VMEM((SLOTS, TILE, half), low),
            pltpu.VMEM((8, TILE, half), low),
            pltpu.VMEM((2, 4, 4, 2, 32, half), low),
            pltpu.VMEM((3, 2, 4, 2, 32, 384), low),
            pltpu.VMEM((3, 2, 4, 2, 32, 384), low),
            pltpu.VMEM((3, 4, 4, 32, 256), low),
            pltpu.VMEM((4, 2, 2, 32, 384), low),
            pltpu.VMEM((2, 2, 4, 32, 384), low),
            pltpu.VMEM((4, 4, 32, 256), low),
            pltpu.VMEM((3, 2, 2, 32, 384), low),
            pltpu.VMEM((3, 4, 32, 384), low),
            pltpu.VMEM((3, 4, 32, 256), low),
            pltpu.VMEM((2, 2, 32, 384), full),
            pltpu.VMEM((4, 32, 384), full),
            pltpu.VMEM((4, 32, 256), full),
            pltpu.VMEM((3, 32, 384), full),
            pltpu.VMEM((3, 32, 384), full),
            pltpu.VMEM((3, 32, 256), full),
            pltpu.VMEM((32, half), full),
            pltpu.VMEM((16, half), full),
            dma, dma((CHUNKS,)), dma((CHUNKS,)), dma((CHUNKS,)), dma((CHUNKS,)), dma, dma,
            dma((8,)), dma((8,)), dma((8,)), dma((42,)), dma((42,)),
            dma((9,)), dma((9,)), dma((9,)), dma((9,)), dma, dma,
        ],
        compiler_params=pltpu.CompilerParams(
            collective_id=0, has_side_effects=True, vmem_limit_bytes=62 * 2**20),
        name="densities",
    )(occ_energy, vir_energy.reshape(1, virtuals), flat)


def per_device(occ_energy, vir_energy, factors):
    orbitals, virtuals, panel = factors.shape
    flat = factors.reshape(orbitals * virtuals, panel)
    gamma_three, gamma_two = density_call(occ_energy, vir_energy, flat)
    return gamma_three.reshape(orbitals, virtuals, panel), gamma_two


def solution(mesh):
    placed = (P(), P(), P(("occ", "aux"), None, None))
    return jax.shard_map(
        per_device,
        mesh=mesh,
        in_specs=placed,
        out_specs=(P(("occ", "aux"), None, None), P(("occ", "aux"), None)),
        check_vma=False,
    )
```

time: 204 us -> 164 us (0.80)
  Pallas kernels: 198 us -> 157 us
    pallas_call x2 -> x1, Pallas kernels: 198 us -> 157 us  [density_call(): pl.pallas_call(density_kernel, out_shape=(jax.ShapeDtypeStruct((width, pa...]
where the time goes in v3:
time: 164 us
  Pallas kernels  157 us (96%)
  local copies, waits for them, and re-layouts  5.48 us (3%)
    pallas_call x1, Pallas kernels, density_call(): pl.pallas_call(density_kernel, out_shape=(jax.ShapeDtypeStruct((width, pa...  157 us
    unnamed x4, local copies, waits for them, and re-layouts  5.48 us

profile of v3, /device:TPU:1, one launch (start us, length us, event | category | flops | bytes accessed | tf_op | source)
XLA Modules:
  0.0 163.6 jit_solution(17303049767814995655)
XLA Ops:
  0.6 157.5 %densities.1 = (bf16[1024,2048]{1,0:T(8,128)(2,1)}, f32[16,2048]{1,0:T(8,128)}) custom-call(f32[256]{0:T(256)} %occ.1, f32[1,512]{1,0:T(1,128)} %bitcast.5, bf16[1024,2048]{1,0:T(8,128)(2,1)} %bitcast.3), custom_call_target="tpu_custom_call" | custom-call | tf_op jit(solution)/shard_map/densities/pallas_call | solution.py:398
  158.1 0.0 copy-start
  158.1 4.8 %copy.7 = bf16[2,512,2048]{2,1,0:T(8,128)(2,1)} copy(bf16[2,512,2048]{2,1,0:T(8,128)(2,1)} %bitcast.4) | data formatting | bytes 8388608
  163.0 0.0 copy-done
  163.0 0.7 copy.8
Async XLA Ops:
  158.1 4.8 %copy-start = (f32[16,2048]{1,0:T(8,128)S(1)}, f32[16,2048]{1,0:T(8,128)}, u32[]{:S(2)}) copy-start(f32[16,2048]{1,0:T(8,128)} %get-tuple-element.9) | copy-start | bytes 393220

commit v4 on v3

v4 whole, which is shorter than its diff:
```python
import jax
import jax.numpy as jnp
from jax import lax
from jax.experimental import pallas as pl
from jax.experimental.pallas import tpu as pltpu
from jax.sharding import PartitionSpec as P

MESH = pl.DeviceIdType.MESH
NT = (((1,), (1,)), ((), ()))
TN = (((0,), (0,)), ((), ()))
SIZES = (64,) * 14 + (32, 32, 32, 16, 16)
STARTS = tuple(sum(SIZES[:c]) for c in range(len(SIZES)))
CHUNKS = len(SIZES)
RELAYS = 16
LAG = 3
TILE = 256
COLS = ((0, 384), (384, 384), (768, 256))
NEAR_FIRST = (2, 1, 3, 0)


def device(position):
    return (position // 2, position % 2)


def by_plane(z, values):
    return jnp.where(z == 0, values[0], jnp.where(z == 1, values[1], jnp.where(z == 2, values[2], values[3])))


def coordinates():
    occ, aux = lax.axis_index("occ"), lax.axis_index("aux")
    return (occ // 8) % 4, (occ // 2) % 4, aux * 2 + occ // 32, occ % 2


def chip(x, y, z, core):
    return ((z % 2) * 32 + x * 8 + y * 2 + core, z // 2)


def density_kernel(
    occ, vir, factors, gamma_out, out, own, near, far, ints, amps, term, base, transit,
    gamma, turned, other_turned, other_own, part,
    first0, first1, first2, mid0, mid1, mid2, second0, second1, second2,
    late0, late1, late2, third0, third1, third2, rows, rows_in,
    load_sem, near_send, near_recv, far_send, far_recv, cross_send, cross_recv,
    transit_send, transit_recv, half_send, half_recv,
    store_sem, core_send, core_recv, send1, recv1, send2, recv2, send3, recv3, end_send, end_recv,
):
    width, panel = own.shape
    virtuals = vir.shape[1]
    strip = width // RELAYS
    count = 2 * lax.axis_size("occ")
    me = lax.axis_index("occ") * 2 + lax.axis_index("aux")
    even = me % 2 == 0
    step = 1 - 2 * (me % 2)
    near_block = (me + step + count) % count
    far_block = (me - step + count) % count
    onward = (me + 2 * step + count) % count
    behind = (me - 2 * step + count) % count

    x, y, z, core = coordinates()
    column = jnp.where(z < 2, x * 4 + y, 15 - (x * 4 + y))
    ends = me % 64 == jnp.where(even, 62, 1)
    crosses = (me % 64 == 0) | (me % 64 == 63)
    direct_far = jnp.logical_not(crosses)
    relays = core == jnp.where(z < 2, 1, 0)
    relay_from = by_plane(z, (127, 63, 64, 0))
    relay_to = by_plane(z, (0, 64, 63, 127))

    def relay_of(c, plane):
        at = jnp.where(plane < 2, c * 2 + 1, (RELAYS - 1 - c) * 2)
        return ((plane % 2) * 32 + at, plane // 2)

    plane_on = by_plane(z, (3, 2, 1, 0))

    z_lo, z_hi = z % 2, z // 2
    half = panel // 2
    mine = pl.multiple_of(core * half, half)
    others = pl.multiple_of((1 - core) * half, half)
    scale = float(count * width) ** (-0.5)

    def along(axis, by):
        place = [x, y, z]
        place[axis] = (place[axis] + by) % 4
        return chip(*place, core)

    def remote(src, dst, send, recv, target):
        return pltpu.make_async_remote_copy(
            src_ref=src, dst_ref=dst, send_sem=send, recv_sem=recv,
            device_id=target, device_id_type=MESH)

    load = pltpu.make_async_copy(factors, own, load_sem)
    load.start()

    barrier = pltpu.get_barrier_semaphore()
    for other in (near_block, onward, behind):
        pl.semaphore_signal(barrier, inc=1, device_id=device(other), device_id_type=MESH)
    for axis in range(3):
        for by in (1, 2, 3):
            pl.semaphore_signal(barrier, inc=1, device_id=along(axis, by), device_id_type=MESH)
    pl.semaphore_signal(barrier, inc=1, device_id=chip(x, y, z, 1 - core), device_id_type=MESH)

    @pl.when(crosses)
    def _():
        for c in range(RELAYS):
            pl.semaphore_signal(barrier, inc=1, device_id=relay_of(c, z), device_id_type=MESH)

    @pl.when(relays)
    def _():
        pl.semaphore_signal(barrier, inc=1, device_id=device(relay_from), device_id_type=MESH)

    pl.semaphore_wait(barrier, 13 + jnp.where(crosses, RELAYS, 0) + jnp.where(relays, 1, 0))

    def span(c):
        return pl.ds(STARTS[c], SIZES[c])

    def strip_at(k):
        return pl.ds(k * strip, strip)

    direct = [
        pltpu.make_async_remote_copy(
            src_ref=factors.at[span(c)], dst_ref=near.at[span(c)],
            send_sem=near_send.at[c], recv_sem=near_recv.at[c],
            device_id=device(near_block), device_id_type=MESH)
        for c in range(CHUNKS)
    ]
    passed = [
        pltpu.make_async_remote_copy(
            src_ref=near.at[span(c)], dst_ref=far.at[span(c)],
            send_sem=far_send.at[c], recv_sem=far_recv.at[c],
            device_id=device(onward), device_id_type=MESH)
        for c in range(CHUNKS)
    ]
    crossing = [
        pltpu.make_async_remote_copy(
            src_ref=factors.at[strip_at(k)], dst_ref=transit,
            send_sem=cross_send.at[k], recv_sem=transit_recv,
            device_id=relay_of(k, plane_on), device_id_type=MESH)
        for k in range(RELAYS)
    ]
    landing = [
        pltpu.make_async_remote_copy(
            src_ref=transit, dst_ref=far.at[strip_at(k)],
            send_sem=transit_send, recv_sem=cross_recv.at[k],
            device_id=device(relay_to), device_id_type=MESH)
        for k in range(RELAYS)
    ]
    relayed = pltpu.make_async_remote_copy(
        src_ref=transit, dst_ref=far.at[pl.ds(pl.multiple_of(column * strip, strip), strip)],
        send_sem=transit_send, recv_sem=cross_recv.at[column],
        device_id=device(relay_to), device_id_type=MESH)
    for copy in direct:
        copy.start()
    half_swap = remote(factors.at[:, pl.ds(others, half)], other_own, half_send, half_recv, chip(x, y, z, 1 - core))
    half_swap.start()

    def relay(k):
        @pl.when(relays & (column == k))
        def _():
            crossing[k].wait_recv()
            relayed.start()

    row = jnp.broadcast_to(vir[...], (virtuals, virtuals))
    base[...] = row + row.T
    load.wait()

    def pair_ints(block, which, piece):
        left = piece % 2 * TILE

        @pl.loop(0, width // 512)
        def _(r):
            at = pl.ds(pl.multiple_of(r * 512, 512), 512)
            ints[which, at, left:left + TILE] = lax.dot_general(
                own[at, :], block[piece * TILE:(piece + 1) * TILE, :], NT,
                preferred_element_type=jnp.float32)

    def pair_amps(which, other, n):
        other_energy = occ[2 * other + n]
        for i in range(2):
            energy = occ[2 * me + i]
            for a in range(virtuals // TILE):
                for b in range(virtuals // TILE):
                    top, side = i * virtuals + a * TILE, i * virtuals + b * TILE
                    here = ints[which, top:top + TILE, b * TILE:(b + 1) * TILE]
                    swapped = ints[which, side:side + TILE, a * TILE:(a + 1) * TILE].T
                    gap = base[a * TILE:(a + 1) * TILE, b * TILE:(b + 1) * TILE] - energy - other_energy
                    amps[which, top:top + TILE, b * TILE:(b + 1) * TILE] = (
                        (2.0 * here - swapped) / gap).astype(jnp.bfloat16)

    def pair_term(which, block, n, first=False):
        @pl.loop(0, width // 512)
        def _(r):
            at = pl.ds(pl.multiple_of(r * 512, 512), 512)
            for c in range(0, panel, 512):
                value = jnp.dot(
                    amps[which, at, :], block[n * virtuals:(n + 1) * virtuals, c:c + 512],
                    preferred_element_type=jnp.float32)
                if not first:
                    value += term[at, c:c + 512]
                term[at, c:c + 512] = value

    def far_piece(piece):
        @pl.when(crosses)
        def _():
            for k in range(piece * 4, piece * 4 + 4):
                landing[k].wait_recv()

        pair_ints(far, 1, piece)
        if piece % 2 == 1:
            pair_amps(1, far_block, piece // 2)
        if piece == 1:
            pair_term(1, far, 0)

    def near_piece(piece):
        pair_ints(near, 0, piece)
        if piece % 2 == 1:
            pair_amps(0, near_block, piece // 2)
            pair_term(0, near, piece // 2, first=piece == 1)

    ends_of = {STARTS[c] + SIZES[c]: c for c in range(CHUNKS)}
    whole = {ends_of[(p + 1) * TILE]: p for p in range(width // TILE)}
    for c in range(CHUNKS):
        direct[c].wait_recv()
        pl.when(jnp.logical_not(ends))(passed[c].start)
        if 2 * c < RELAYS:
            pl.when(crosses)(crossing[2 * c].start)
            pl.when(crosses)(crossing[2 * c + 1].start)
        if 0 <= 2 * (c - 3) < RELAYS:
            relay(2 * (c - 3))
            relay(2 * (c - 3) + 1)
        if c >= LAG:
            pl.when(direct_far)(passed[c - LAG].wait_recv)
            if c - LAG in whole:
                far_piece(whole[c - LAG])
        if c in whole:
            near_piece(whole[c])
    for c in range(CHUNKS - LAG, CHUNKS):
        pl.when(direct_far)(passed[c].wait_recv)
    far_piece(3)

    tiles = [(e, d) for d in NEAR_FIRST for e in (1, 0)]
    swaps = []
    stores = []
    waits = [[], [], []]

    def columns(t):
        e, d = tiles[t]
        zl, xt = (z_lo + e) % 2, (x + d) % 4
        return zl, xt, pl.ds(pl.multiple_of((zl * 4 + xt) * TILE, TILE), TILE)

    def tile_term(t):
        _, _, at = columns(t)
        for r in range(0, width, 512):
            value = term[r:r + 512, at] + jnp.dot(
                amps[1, r:r + 512, :], far[virtuals:width, at], preferred_element_type=jnp.float32)
            value = value.astype(jnp.bfloat16)
            gamma[r:r + 512, at] = value
            turned[t, :, r:r + 512] = value.T
        store = pltpu.make_async_copy(gamma.at[:, at], gamma_out.at[:, at], store_sem.at[t])
        store.start()
        stores.append(store)
        swap = remote(turned.at[t], other_turned.at[t], core_send.at[t], core_recv.at[t], chip(x, y, z, 1 - core))
        swap.start()
        swaps.append(swap)

    def finish(t):
        e, d = tiles[t]
        zl, xt, _ = columns(t)
        swaps[t].wait_recv()
        for c in range(0, half, 512):
            total = jnp.dot(
                turned[t], own[:, pl.ds(pl.multiple_of(mine + c, 512), 512)], preferred_element_type=jnp.float32)
            total += jnp.dot(other_turned[t], other_own[:, c:c + 512], preferred_element_type=jnp.float32)
            total = (total * scale).astype(jnp.bfloat16)
            for yy in range(4):
                for cc in range(2):
                    for zh in range(2):
                        at = ((yy * 2 + cc) * 2 + zh) * 16
                        part[zl, xt, yy, zh, cc * 16:(cc + 1) * 16, c:c + 512] = total[at:at + 16, :]
        copies = []
        if d:
            cols = pl.ds(*COLS[0])
            copies.append((0, part.at[zl, xt, :, :, :, cols], first0.at[d - 1, zl], along(0, d)))
        for by in (2, 1, 3):
            cols = pl.ds(*COLS[1])
            copies.append((1, part.at[zl, xt, (y + by) % 4, :, :, cols], first1.at[by - 1, zl, xt], along(1, by)))
        for by in ((1, 3) if e else (2,)):
            cols = pl.ds(*COLS[2])
            copies.append((2, part.at[zl, xt, :, ((z + by) % 4) // 2, :, cols], first2.at[by - 1, xt], along(2, by)))
        for k, src, dst, target in copies:
            n = sum(len(w) for w in waits)
            copy = remote(src, dst, send1.at[n], recv1.at[n], target)
            copy.start()
            waits[k].append(copy)

    half_swap.wait_recv()
    for t in range(len(tiles)):
        tile_term(t)
        if t:
            finish(t - 1)
    finish(len(tiles) - 1)

    def wide(value):
        return value.astype(jnp.float32)

    seconds = [[], [], []]

    def second(k, by, src, dst, axis):
        n = k * 3 + by - 1
        copy = remote(src, dst, send2.at[n], recv2.at[n], along(axis, by))
        copy.start()
        seconds[k].append(copy)

    for copy in waits[0]:
        copy.wait_recv()
    for zl in range(2):
        for yy in range(4):
            for zh in range(2):
                total = wide(part[zl, x, yy, zh, :, 0:384])
                for j in range(3):
                    total += wide(first0[j, zl, yy, zh])
                mid0[yy, zl, zh] = total.astype(mid0.dtype)
    for by in (2, 1, 3):
        second(0, by, mid0.at[(y + by) % 4], second0.at[by - 1], 1)

    for copy in waits[1]:
        copy.wait_recv()
    for zl in range(2):
        for xx in range(4):
            for zh in range(2):
                total = wide(part[zl, xx, y, zh, :, 384:768])
                for j in range(3):
                    total += wide(first1[j, zl, xx, zh])
                mid1[zl, zh, xx] = total.astype(mid1.dtype)
    for by in (2, 1, 3):
        far = (z + by) % 4
        second(1, by, mid1.at[far % 2, far // 2], second1.at[by - 1], 2)

    for copy in waits[2]:
        copy.wait_recv()
    for xx in range(4):
        for yy in range(4):
            total = wide(part[z_lo, xx, yy, z_hi, :, 768:1024])
            for j in range(3):
                total += wide(first2[j, xx, yy])
            mid2[xx, yy] = total.astype(mid2.dtype)
    for by in (2, 1, 3):
        second(2, by, mid2.at[(x + by) % 4], second2.at[by - 1], 0)

    thirds = [[], [], []]

    def third(k, by, src, dst, axis):
        n = k * 3 + by - 1
        copy = remote(src, dst, send3.at[n], recv3.at[n], along(axis, by))
        copy.start()
        thirds[k].append(copy)

    for copy in seconds[0]:
        copy.wait_recv()
    for zl in range(2):
        for zh in range(2):
            total = wide(mid0[y, zl, zh])
            for j in range(3):
                total += wide(second0[j, zl, zh])
            late0[zl, zh] = total.astype(jnp.bfloat16)
    for by in (2, 1, 3):
        far = (z + by) % 4
        third(0, by, late0.at[far % 2, far // 2], third0.at[by - 1], 2)

    for copy in seconds[1]:
        copy.wait_recv()
    for xx in range(4):
        total = wide(mid1[z_lo, z_hi, xx])
        for j in range(3):
            total += wide(second1[j, xx])
        late1[xx] = total.astype(jnp.bfloat16)
    for by in (2, 1, 3):
        third(1, by, late1.at[(x + by) % 4], third1.at[by - 1], 0)

    for copy in seconds[2]:
        copy.wait_recv()
    for yy in range(4):
        total = wide(mid2[x, yy])
        for j in range(3):
            total += wide(second2[j, yy])
        late2[yy] = total.astype(jnp.bfloat16)
    for by in (2, 1, 3):
        third(2, by, late2.at[(y + by) % 4], third2.at[by - 1], 1)

    for k in range(3):
        for copy in thirds[k]:
            copy.wait_recv()
    def last_sum(late, slots):
        return wide(late) + wide(slots[0]) + wide(slots[1]) + wide(slots[2])

    rows[:, 0:384] = last_sum(late0[z_lo, z_hi], third0)
    rows[:, 384:768] = last_sum(late1[x], third1)
    rows[:, 768:1024] = last_sum(late2[y], third2)
    last = remote(
        rows.at[pl.ds(pl.multiple_of((1 - core) * 16, 16), 16)], rows_in, end_send, end_recv,
        chip(x, y, z, 1 - core))
    last.start()
    out[:, pl.ds(mine, half)] = rows[pl.ds(pl.multiple_of(core * 16, 16), 16), :]
    last.wait_recv()
    out[:, pl.ds(others, half)] = rows_in[...]

    for copy in direct + [half_swap]:
        copy.wait_send()
    for copy in passed:
        pl.when(jnp.logical_not(ends))(copy.wait_send)
    for copy in crossing:
        pl.when(crosses)(copy.wait_send)
    pl.when(relays)(relayed.wait_send)
    for store in stores:
        store.wait()
    for copy in swaps + waits[0] + waits[1] + waits[2] + sum(seconds, []) + sum(thirds, []) + [last]:
        copy.wait_send()


def density_call(occ_energy, vir_energy, flat):
    width, panel = flat.shape
    virtuals = vir_energy.shape[0]
    half = panel // 2
    low, full = jnp.bfloat16, jnp.float32
    dma = pltpu.SemaphoreType.DMA
    block = pltpu.VMEM((width, panel), low)
    term = pltpu.VMEM((width, panel), full)
    return pl.pallas_call(
        density_kernel,
        out_shape=(
            jax.ShapeDtypeStruct((width, panel), low),
            jax.ShapeDtypeStruct((16, panel), full),
        ),
        in_specs=[
            pl.BlockSpec(memory_space=pltpu.SMEM),
            pl.BlockSpec(memory_space=pltpu.VMEM),
            pl.BlockSpec(memory_space=pl.ANY),
        ],
        out_specs=(pl.BlockSpec(memory_space=pl.ANY), pl.BlockSpec(memory_space=pltpu.VMEM)),
        scratch_shapes=[
            block, block, block,
            pltpu.VMEM((2, width, virtuals), full),
            pltpu.VMEM((2, width, virtuals), low),
            term,
            pltpu.VMEM((virtuals, virtuals), full),
            pltpu.VMEM((width // RELAYS, panel), low),
            block,
            pltpu.VMEM((panel // TILE, TILE, width), low),
            pltpu.VMEM((panel // TILE, TILE, width), low),
            pltpu.VMEM((width, half), low),
            pltpu.VMEM((2, 4, 4, 2, 32, half), low),
            pltpu.VMEM((3, 2, 4, 2, 32, 384), low),
            pltpu.VMEM((3, 2, 4, 2, 32, 384), low),
            pltpu.VMEM((3, 4, 4, 32, 256), low),
            pltpu.VMEM((4, 2, 2, 32, 384), low),
            pltpu.VMEM((2, 2, 4, 32, 384), low),
            pltpu.VMEM((4, 4, 32, 256), low),
            pltpu.VMEM((3, 2, 2, 32, 384), low),
            pltpu.VMEM((3, 4, 32, 384), low),
            pltpu.VMEM((3, 4, 32, 256), low),
            pltpu.VMEM((2, 2, 32, 384), low),
            pltpu.VMEM((4, 32, 384), low),
            pltpu.VMEM((4, 32, 256), low),
            pltpu.VMEM((3, 32, 384), low),
            pltpu.VMEM((3, 32, 384), low),
            pltpu.VMEM((3, 32, 256), low),
            pltpu.VMEM((32, half), full),
            pltpu.VMEM((16, half), full),
            dma, dma((CHUNKS,)), dma((CHUNKS,)), dma((CHUNKS,)), dma((CHUNKS,)), dma((RELAYS,)), dma((RELAYS,)),
            dma, dma, dma, dma,
            dma((8,)), dma((8,)), dma((8,)), dma((42,)), dma((42,)),
            dma((9,)), dma((9,)), dma((9,)), dma((9,)), dma, dma,
        ],
        compiler_params=pltpu.CompilerParams(
            collective_id=0, has_side_effects=True, vmem_limit_bytes=62 * 2**20),
        name="densities",
    )(occ_energy, vir_energy.reshape(1, virtuals), flat)


def hand_over_kernel(three, two, three_out, two_out):
    three_out[...] = three[...]
    two_out[...] = two[...]


def hand_over(three, two):
    part = pl.BlockSpec((three.shape[0] // 8, three.shape[1]), lambda i: (i, 0))
    whole = pl.BlockSpec(two.shape, lambda i: (0, 0))
    return pl.pallas_call(
        hand_over_kernel,
        out_shape=(
            jax.ShapeDtypeStruct(three.shape, three.dtype),
            jax.ShapeDtypeStruct(two.shape, two.dtype),
        ),
        grid=(8,),
        in_specs=[part, whole],
        out_specs=(part, whole),
        name="hand_over",
    )(three, two)


def per_device(occ_energy, vir_energy, factors):
    orbitals, virtuals, panel = factors.shape
    flat = factors.reshape(orbitals * virtuals, panel)
    gamma_three, gamma_two = density_call(occ_energy, vir_energy, flat)
    gamma_three, gamma_two = hand_over(gamma_three, gamma_two)
    return gamma_three.reshape(orbitals, virtuals, panel), gamma_two


def solution(mesh):
    placed = (P(), P(), P(("occ", "aux"), None, None))
    return jax.shard_map(
        per_device,
        mesh=mesh,
        in_specs=placed,
        out_specs=(P(("occ", "aux"), None, None), P(("occ", "aux"), None)),
        check_vma=False,
    )
```

time: 164 us -> 161 us (0.982)
  local copies, waits for them, and re-layouts: 5.48 us -> 0 us
  Pallas kernels: 157 us -> 160 us
    pallas_call x0 -> x1, Pallas kernels: none -> 6.67 us  [hand_over(): pl.pallas_call(hand_over_kernel, out_shape=(jax.ShapeDtypeStruct(three.sh...]
    unnamed x4 -> x0, local copies, waits for them, and re-layouts: 5.48 us -> none
    pallas_call x1, Pallas kernels: 157 us -> 154 us  [density_call(): pl.pallas_call(density_kernel, out_shape=(jax.ShapeDtypeStruct((width, pa...]
where the time goes in v4:
time: 161 us
  Pallas kernels  160 us (99%)
    pallas_call x1, Pallas kernels, density_call(): pl.pallas_call(density_kernel, out_shape=(jax.ShapeDtypeStruct((width, pa...  154 us
    pallas_call x1, Pallas kernels, hand_over(): pl.pallas_call(hand_over_kernel, out_shape=(jax.ShapeDtypeStruct(three.sh...  6.67 us

profile of v4, /device:TPU:1, one launch (start us, length us, event | category | flops | bytes accessed | tf_op | source)
XLA Modules:
  0.0 161.1 jit_solution(17538151262815669843)
XLA Ops:
  0.6 153.8 %densities.1 = (bf16[1024,2048]{1,0:T(8,128)(2,1)}, f32[16,2048]{1,0:T(8,128)}) custom-call(f32[256]{0:T(256)} %occ.1, f32[1,512]{1,0:T(1,128)} %bitcast.4, bf16[1024,2048]{1,0:T(8,128)(2,1)} %bitcast.3), custom_call_target="tpu_custom_call" | custom-call | tf_op jit(solution)/shard_map/densities/pallas_call | solution.py:426
  154.4 6.7 %hand_over.1 = (bf16[1024,2048]{1,0:T(8,128)(2,1)}, f32[16,2048]{1,0:T(8,128)}) custom-call(bf16[1024,2048]{1,0:T(8,128)(2,1)} %get-tuple-element.6.three, f32[16,2048]{1,0:T(8,128)} %get-tuple-element.7.two), custom_call_target="tpu_custom_call" | custom-call | tf_op jit(solution)/shard_map/hand_over/pallas_call | solution.py:486

commit v5 on v4

--- a/solution.py
+++ b/solution.py
@@ -13,6 +13,7 @@
 CHUNKS = len(SIZES)
 RELAYS = 16
 LAG = 3
+RELAY_LAG = 5
 TILE = 256
 COLS = ((0, 384), (384, 384), (768, 256))
 NEAR_FIRST = (2, 1, 3, 0)
@@ -223,9 +224,9 @@
         if 2 * c < RELAYS:
             pl.when(crosses)(crossing[2 * c].start)
             pl.when(crosses)(crossing[2 * c + 1].start)
-        if 0 <= 2 * (c - 3) < RELAYS:
-            relay(2 * (c - 3))
-            relay(2 * (c - 3) + 1)
+        if 0 <= 2 * (c - RELAY_LAG) < RELAYS:
+            relay(2 * (c - RELAY_LAG))
+            relay(2 * (c - RELAY_LAG) + 1)
         if c >= LAG:
             pl.when(direct_far)(passed[c - LAG].wait_recv)
             if c - LAG in whole:
@@ -475,23 +476,39 @@
     )(occ_energy, vir_energy.reshape(1, virtuals), flat)
 
 
-def hand_over_kernel(three, two, three_out, two_out):
-    three_out[...] = three[...]
-    two_out[...] = two[...]
+def hand_over_kernel(three, two, three_out, two_out, block, small, in_sem, out_sem):
+    size = block.shape[0] // 8
+    pieces = [(three.at[pl.ds(p * size, size)], block.at[pl.ds(p * size, size)], three_out.at[pl.ds(p * size, size)])
+              for p in range(8)]
+    pieces.append((two, small, two_out))
+    reads = [pltpu.make_async_copy(src, held, in_sem.at[p]) for p, (src, held, _) in enumerate(pieces)]
+    writes = [pltpu.make_async_copy(held, dst, out_sem.at[p]) for p, (_, held, dst) in enumerate(pieces)]
+    for copy in reads:
+        copy.start()
+    for read, write in zip(reads, writes):
+        read.wait()
+        write.start()
+    for copy in writes:
+        copy.wait()
 
 
 def hand_over(three, two):
-    part = pl.BlockSpec((three.shape[0] // 8, three.shape[1]), lambda i: (i, 0))
-    whole = pl.BlockSpec(two.shape, lambda i: (0, 0))
+    anywhere = pl.BlockSpec(memory_space=pl.ANY)
     return pl.pallas_call(
         hand_over_kernel,
         out_shape=(
             jax.ShapeDtypeStruct(three.shape, three.dtype),
             jax.ShapeDtypeStruct(two.shape, two.dtype),
         ),
-        grid=(8,),
-        in_specs=[part, whole],
-        out_specs=(part, whole),
+        in_specs=[anywhere] * 2,
+        out_specs=(anywhere, anywhere),
+        scratch_shapes=[
+            pltpu.VMEM(three.shape, three.dtype),
+            pltpu.VMEM(two.shape, two.dtype),
+            pltpu.SemaphoreType.DMA((9,)),
+            pltpu.SemaphoreType.DMA((9,)),
+        ],
+        compiler_params=pltpu.CompilerParams(vmem_limit_bytes=62 * 2**20),
         name="hand_over",
     )(three, two)
 

time: 161 us -> 154 us (0.957)
  Pallas kernels: 160 us -> 153 us
    pallas_call x1, Pallas kernels: 154 us -> 149 us  [density_call(): pl.pallas_call(density_kernel, out_shape=(jax.ShapeDtypeStruct((width, pa...]
    pallas_call x1, Pallas kernels: 6.67 us -> 3.63 us  [hand_over(): pl.pallas_call(hand_over_kernel, out_shape=(jax.ShapeDtypeStruct(three.sh...]
where the time goes in v5:
time: 154 us
  Pallas kernels  153 us (99%)
    pallas_call x1, Pallas kernels, density_call(): pl.pallas_call(density_kernel, out_shape=(jax.ShapeDtypeStruct((width, pa...  149 us
    pallas_call x1, Pallas kernels, hand_over(): pl.pallas_call(hand_over_kernel, out_shape=(jax.ShapeDtypeStruct(three.sh...  3.63 us

profile of v5, /device:TPU:1, one launch (start us, length us, event | category | flops | bytes accessed | tf_op | source)
XLA Modules:
  0.0 153.7 jit_solution(15923282765734999908)
XLA Ops:
  0.6 149.2 %densities.1 = (bf16[1024,2048]{1,0:T(8,128)(2,1)}, f32[16,2048]{1,0:T(8,128)}) custom-call(f32[256]{0:T(256)} %occ.1, f32[1,512]{1,0:T(1,128)} %bitcast.4, bf16[1024,2048]{1,0:T(8,128)(2,1)} %bitcast.3), custom_call_target="tpu_custom_call" | custom-call | tf_op jit(solution)/shard_map/densities/pallas_call | solution.py:427
  149.9 3.6 %hand_over.1 = (bf16[1024,2048]{1,0:T(8,128)(2,1)}, f32[16,2048]{1,0:T(8,128)}) custom-call(bf16[1024,2048]{1,0:T(8,128)(2,1)} %get-tuple-element.6.three, f32[16,2048]{1,0:T(8,128)} %get-tuple-element.7.two), custom_call_target="tpu_custom_call" | custom-call | tf_op jit(solution)/shard_map/hand_over/pallas_call | solution.py:497

commit v6 on v5

--- a/solution.py
+++ b/solution.py
@@ -12,7 +12,7 @@
 STARTS = tuple(sum(SIZES[:c]) for c in range(len(SIZES)))
 CHUNKS = len(SIZES)
 RELAYS = 16
-LAG = 3
+LAG = 5
 RELAY_LAG = 5
 TILE = 256
 COLS = ((0, 384), (384, 384), (768, 256))

time: 154 us -> 156 us (1.013)
  Pallas kernels: 153 us -> 155 us
    pallas_call x1, Pallas kernels: 149 us -> 152 us  [density_call(): pl.pallas_call(density_kernel, out_shape=(jax.ShapeDtypeStruct((width, pa...]
where the time goes in v6:
time: 156 us
  Pallas kernels  155 us (99%)
    pallas_call x1, Pallas kernels, density_call(): pl.pallas_call(density_kernel, out_shape=(jax.ShapeDtypeStruct((width, pa...  152 us
    pallas_call x1, Pallas kernels, hand_over(): pl.pallas_call(hand_over_kernel, out_shape=(jax.ShapeDtypeStruct(three.sh...  3.63 us

profile of v6, /device:TPU:1, one launch (start us, length us, event | category | flops | bytes accessed | tf_op | source)
XLA Modules:
  0.0 155.9 jit_solution(3819985638450537548)
XLA Ops:
  0.6 151.5 %densities.1 = (bf16[1024,2048]{1,0:T(8,128)(2,1)}, f32[16,2048]{1,0:T(8,128)}) custom-call(f32[256]{0:T(256)} %occ.1, f32[1,512]{1,0:T(1,128)} %bitcast.4, bf16[1024,2048]{1,0:T(8,128)(2,1)} %bitcast.3), custom_call_target="tpu_custom_call" | custom-call | tf_op jit(solution)/shard_map/densities/pallas_call | solution.py:427
  152.2 3.6 %hand_over.1 = (bf16[1024,2048]{1,0:T(8,128)(2,1)}, f32[16,2048]{1,0:T(8,128)}) custom-call(bf16[1024,2048]{1,0:T(8,128)(2,1)} %get-tuple-element.6.three, f32[16,2048]{1,0:T(8,128)} %get-tuple-element.7.two), custom_call_target="tpu_custom_call" | custom-call | tf_op jit(solution)/shard_map/hand_over/pallas_call | solution.py:497
